TPU v7x, 32 devices: a whole 2x2x4 slice. The times are simulated.
32 devices in a mesh: groups: 2 (over y), owner: 8 (over z, x), tile: 2 (over core).
Axes of the slice: x: 2, y: 2, z: 4, core: 2. Of those that a mesh axis runs over, the one named last changes fastest.
Arguments:
- embeddings: bfloat16 [8192, 1024], P(('groups', 'owner', 'tile')), parts along dimension 0, may hold values from -6 to 6
- cluster_of: int32 [8192], P(('groups', 'owner', 'tile')), parts along dimension 0, may hold values from 0 to 15, as said below
- rank_of: int32 [8192], P(('groups', 'owner', 'tile')), parts along dimension 0, may hold values from 0 to 511, as said below
Outputs:
- max_similarity: float32 [8192], P(('groups', 'owner', 'tile')), parts along dimension 0
There are 2 independent parts, one for each index of `groups`. A program takes and returns all parts, laid end to end along the dimension named above; each array names one. Nothing has to cross between parts.
Inputs may be any that keep to these rules, and one draw needn't show every extreme that they name: `cluster_of`: in each aligned block of 256 rows (the rows of one device) no cluster is named more than 32 times; one cluster is named exactly 32 times in every block, so that it holds 512 rows. `rank_of`: within each cluster the ranks of its rows are 0 to its size minus 1, each once; cluster ids, ranks and sizes as given by cluster_of.
All inputs are finite; a program needn't handle non-finite values.
Results may differ from a plain program's by a relative error of at most 0.0013.
Values may be sent and summed in bfloat16 or wider, within the bound.
A program may use at most 64 MiB of HBM per device.

v0:
```python
import jax
import jax.numpy as jnp
from jax import lax
from jax.sharding import PartitionSpec as P

CL_OWN = 2


EPSILON = 1e-06


def normalize_rows(embeddings):
    as_float = embeddings.astype(jnp.float32)
    total = jnp.sum(as_float * as_float, axis=1, keepdims=True)
    return (as_float * lax.rsqrt(total + EPSILON)).astype(jnp.bfloat16)


def place_rows(arrived_rows, arrived_ranks, longest):
    local_count = arrived_rows.shape[1]
    feature_width = arrived_rows.shape[3]
    cluster_index = jnp.broadcast_to(
        jnp.arange(local_count, dtype=jnp.int32)[None, :, None], arrived_ranks.shape
    )
    ordered = jnp.zeros((local_count, longest, feature_width), jnp.bfloat16)
    ordered = ordered.at[cluster_index, arrived_ranks].set(arrived_rows, mode="drop")
    live_rows = jnp.sum((arrived_ranks < longest).astype(jnp.int32), axis=(0, 2))
    return (ordered, live_rows)


def lookup_maxima(maxima, ranks, longest):
    cluster_index = jnp.broadcast_to(
        jnp.arange(maxima.shape[0], dtype=jnp.int32)[None, :, None], ranks.shape
    )
    return maxima[cluster_index, jnp.minimum(ranks, longest - 1)]


def block_maxima(ordered_rows, first, count, block_rows):
    query_rows = lax.dynamic_slice_in_dim(ordered_rows, 0 + first, count, 0)
    scores = jnp.einsum("qd,kd->qk", query_rows, ordered_rows, preferred_element_type=jnp.float32)
    query_pos = 0 + first + jnp.arange(count, dtype=jnp.int32)
    key_pos = jnp.arange(block_rows, dtype=jnp.int32)
    masked = jnp.where(key_pos[None, :] < query_pos[:, None], scores, -1.0)
    row_best = jnp.max(masked, axis=1)
    results = [row_best]
    return jnp.stack(results)


def local(embeddings, cluster_of, rank_of):
    row_count, feature_width = embeddings.shape
    owner_count = lax.axis_size("owner")
    core_count = lax.axis_size("tile")
    cluster_count = CL_OWN * owner_count
    capacity = 2 * row_count // cluster_count
    longest = owner_count * core_count * capacity
    block_rows = 512
    normed = normalize_rows(embeddings)
    member = (cluster_of[:, None] == jnp.arange(cluster_count, dtype=jnp.int32)[None, :]).astype(
        jnp.bfloat16
    )
    row_ids = jnp.arange(row_count, dtype=jnp.int32)
    earlier = (row_ids[:, None] > row_ids[None, :]).astype(jnp.bfloat16)
    seen = jnp.dot(earlier, member, preferred_element_type=jnp.float32)
    occurrence = jnp.sum(seen * member.astype(jnp.float32), axis=1).astype(jnp.int32)
    slot_index = cluster_of * capacity + occurrence
    outgoing = (
        jnp.zeros((cluster_count * capacity, feature_width), jnp.bfloat16)
        .at[slot_index]
        .set(normed)
    )
    outgoing_ranks = (
        jnp.full((cluster_count * capacity,), longest, jnp.int32).at[slot_index].set(rank_of)
    )
    outgoing = outgoing.reshape(owner_count, CL_OWN, capacity, feature_width)
    outgoing_ranks = outgoing_ranks.reshape(owner_count, CL_OWN, capacity)
    arrived, arrived_ranks = (
        lax.all_to_all(outgoing, "owner", split_axis=0, concat_axis=0, tiled=True),
        lax.all_to_all(outgoing_ranks, "owner", split_axis=0, concat_axis=0, tiled=True),
    )
    everything, every_rank = (
        lax.all_gather(arrived, "tile", axis=0, tiled=True),
        lax.all_gather(arrived_ranks, "tile", axis=0, tiled=True),
    )
    ordered, live_rows = place_rows(everything, every_rank, longest)
    share = block_rows // core_count
    first = lax.axis_index("tile") * share
    halves = jnp.stack(
        [
            block_maxima(ordered[local_index], first, share, block_rows)
            for local_index in range(CL_OWN)
        ]
    )
    whole = lax.all_gather(halves[:, :, None, :], "tile", axis=2, tiled=True)
    maxima = whole.reshape(CL_OWN, longest)
    answers = lookup_maxima(maxima, arrived_ranks, longest)
    returned = lax.all_to_all(answers, "owner", split_axis=0, concat_axis=0, tiled=True)
    return returned.reshape(cluster_count * capacity)[slot_index]


def solution(mesh):
    in_specs = (
        P(("groups", "owner", "tile"), None),
        P(("groups", "owner", "tile")),
        P(("groups", "owner", "tile")),
    )
    out_specs = P(("groups", "owner", "tile"))
    return jax.shard_map(local, mesh=mesh, in_specs=in_specs, out_specs=out_specs, check_vma=False)
```

profile of v0, /device:TPU:0, one launch (start us, length us, event | category | flops | bytes accessed | tf_op | source)
XLA Modules:
  0.0 93.8 jit_solution(11453699134182329262)
XLA Ops:
  6.5 0.0 all-gather.3.cloned.1.call-start
  6.5 1.2 %fusion.3 = f32[256]{0:T(256)S(1)} fusion(bf16[256,1024]{1,0:T(8,128)(2,1)} %param.3), kind=kLoop, calls=%fused_computation.13 | loop fusion | flops 786176 | bytes 525312 | tf_op jit(solution)/shard_map/reduce_sum | solution.py:14
  7.8 1.0 %fusion.2 = f32[256]{0:T(256)S(1)} fusion(s32[256]{0:T(256)} %param.4), kind=kOutput, calls=%fused_computation.12 | convolution fusion | flops 2187008 | bytes 2048 | tf_op jit(solution)/shard_map/dot_general | solution.py:62
  8.7 0.7 compare_select_fusion.2
  9.4 0.0 copy-start.1
  9.4 0.0 copy-start
  9.4 2.5 %scatter_custom_fusion.1 = bf16[512,1024]{1,0:T(8,128)(2,1)S(1)} fusion(s32[256]{0:T(256)S(1)} %compare_select_fusion.2, bf16[256,1024]{1,0:T(8,128)(2,1)} %param.3, f32[256]{0:T(256)S(1)} %add_rsqrt_fusion, bf16[]{:T(256)} %constant.13.clone.1), kind=kCustom, calls=%fused_computation.17 | custom fusion | flops 786432 | bytes 1573890 | tf_op jit(solution)/shard_map/scatter | solution.py:68
  11.9 32.9 %all_to_all.15 = bf16[8,2,32,1024]{3,2,1,0:T(8,128)(2,1)} all-to-all(bf16[8,2,32,1024]{3,2,1,0:T(8,128)(2,1)S(1)} %bitcast.19), channel_id=1, replica_groups=mesh['groups'=2,'owner'=8,'tile'=2] {'owner'}, dimensions={0} | all-to-all | bytes 2097152 | tf_op jit(solution)/shard_map/all_to_all | solution.py:76
  44.8 0.0 all-gather.3.cloned.1.call-update
  44.9 1.6 %scatter_custom_fusion = s32[512]{0:T(512)S(1)} fusion(s32[256]{0:T(256)S(1)} %compare_select_fusion.2, s32[256]{0:T(256)} %param.5, s32[]{:T(128)} %constant.14.clone.1), kind=kCustom, calls=%fused_computation.42 | custom fusion | bytes 2560 | tf_op jit(solution)/shard_map/scatter | solution.py:71
  46.4 0.7 reshape.25
  47.1 3.6 %all-to-all-start = ((s32[8,2,32]{2,1,0:T(2,128)}), s32[8,2,32]{2,1,0:T(2,128)S(1)}, u32[]{:S(2)}, u32[]{:S(2)}) async-start(s32[8,2,32]{2,1,0:T(2,128)} %reshape.25), calls=%async_computation | async-start | bytes 16384 | tf_op jit(solution)/shard_map/all_to_all | solution.py:77
  50.7 6.5 %all-to-all-done = s32[8,2,32]{2,1,0:T(2,128)S(1)} async-done(((s32[8,2,32]{2,1,0:T(2,128)}), s32[8,2,32]{2,1,0:T(2,128)S(1)}, u32[]{:S(2)}, u32[]{:S(2)}) %all-to-all-start) | async-done | bytes 2080 | tf_op jit(solution)/shard_map/all_to_all | solution.py:77
  57.2 0.1 reshape.41
  57.3 1.8 %all_gather.9 = s32[16,2,32]{2,1,0:T(2,128)S(1)} all-gather(s32[8,2,32]{2,1,0:T(2,128)S(1)} %all-to-all-done), channel_id=1, replica_groups=mesh['groups'=2,'owner'=8,'tile'=2] {'tile'}, dimensions={0}, use_global_device_ids=true | all-gather | bytes 6144 | tf_op jit(solution)/shard_map/all_gather | solution.py:81
  59.1 0.0 copy-done.1
  59.1 0.1 multiply_reduce_fusion
  59.2 0.0 copy-done
  59.2 0.1 and_reduce_fusion
  59.3 0.1 reshape.71
  59.4 0.0 all-gather.3.cloned.1.call-done
  59.4 6.6 %scatter_custom_fusion.2 = bf16[1024,1024]{1,0:T(8,128)(2,1)S(1)} fusion(s32[1024]{0:T(1024)S(1)} %reshape.71, bf16[1024,1024]{1,0:T(8,128)(2,1)} %bitcast.22, bf16[]{:T(256)} %constant.13.clone.1), kind=kCustom, calls=%fused_computation.15 | custom fusion | bytes 2097664
  66.0 0.2 fusion.24
  66.2 0.6 fusion
  66.7 0.6 fusion.1
  67.3 1.8 %all-gather = f32[2,2,256]{2,0,1:T(2,128)S(1)} all-gather(f32[2,1,256]{2,0,1:T(2,128)S(1)} %pad_maximum_fusion), channel_id=2, replica_groups=mesh['groups'=2,'owner'=8,'tile'=2] {'tile'}, dimensions={1}, use_global_device_ids=true | all-gather | bytes 6144 | tf_op jit(solution)/shard_map/all_gather | solution.py:92
  69.1 4.8 %gather_fusion = f32[512]{0:T(512)S(1)} fusion(f32[2,512]{1,0:T(2,128)S(1)} %bitcast.18, s32[512]{0:T(512)S(1)} %reshape.41), kind=kCustom, calls=%fused_computation | custom fusion | bytes 8192 | tf_op jit(solution)/shard_map/gather | solution.py:34
  73.9 0.7 reshape.44
  74.6 3.3 %all-to-all-start.2 = ((f32[8,2,32]{2,1,0:T(2,128)}), f32[8,2,32]{2,1,0:T(2,128)S(1)}, u32[]{:S(2)}, u32[]{:S(2)}) async-start(f32[8,2,32]{2,1,0:T(2,128)} %reshape.44), calls=%async_computation.2 | async-start | bytes 16384 | tf_op jit(solution)/shard_map/all_to_all | solution.py:95
  78.0 6.4 %all-to-all-done.2 = f32[8,2,32]{2,1,0:T(2,128)S(1)} async-done(((f32[8,2,32]{2,1,0:T(2,128)}), f32[8,2,32]{2,1,0:T(2,128)S(1)}, u32[]{:S(2)}, u32[]{:S(2)}) %all-to-all-start.2) | async-done | bytes 2080 | tf_op jit(solution)/shard_map/all_to_all | solution.py:95
  84.4 0.1 reshape.28
  84.5 2.5 %gather_fusion.1 = f32[256]{0:T(256)} fusion(f32[512]{0:T(512)S(1)} %reshape.28, s32[1024]{0:T(1024)S(1)} %pad_clamp_fusion), kind=kCustom, calls=%fused_computation.1 | custom fusion | bytes 3072 | tf_op jit(solution)/shard_map/gather | solution.py:96
  (9 shorter events, 0.1 us)
Async XLA Ops:
  6.5 52.9 %all-gather.3.cloned.1.call-start = ((), (), s32[]{:S(2)}) async-start(), calls=%async_computation.3 | async-start | bytes 3145728 | tf_op jit(solution)/shard_map/all_gather | solution.py:80
  9.4 49.7 %copy-start.1 = (s32[2]{0:T(128)S(1)}, s32[2]{0:T(128)}, u32[]{:S(2)}) copy-start(s32[2]{0:T(128)} %constant.5) | copy-start | bytes 28
  9.4 49.8 %copy-start = (s32[2]{0:T(128)S(1)}, s32[2]{0:T(128)}, u32[]{:S(2)}) copy-start(s32[2]{0:T(128)} %constant.8) | copy-start | bytes 28
  47.1 10.1 %all-to-all-start = ((s32[8,2,32]{2,1,0:T(2,128)}), s32[8,2,32]{2,1,0:T(2,128)S(1)}, u32[]{:S(2)}, u32[]{:S(2)}) async-start(s32[8,2,32]{2,1,0:T(2,128)} %reshape.25), calls=%async_computation | async-start | bytes 16384 | tf_op jit(solution)/shard_map/all_to_all | solution.py:77
  74.6 9.8 %all-to-all-start.2 = ((f32[8,2,32]{2,1,0:T(2,128)}), f32[8,2,32]{2,1,0:T(2,128)S(1)}, u32[]{:S(2)}, u32[]{:S(2)}) async-start(f32[8,2,32]{2,1,0:T(2,128)} %reshape.44), calls=%async_computation.2 | async-start | bytes 16384 | tf_op jit(solution)/shard_map/all_to_all | solution.py:95
Sparse Core Ops, SparseCore 0:
  45.0 9.6 all-gather.2
where the time goes:
time: 94.3 us; the launch traced here: 93.8 us
  blocking collectives  36.5 us (39%)
  local copies, waits for them, and re-layouts  17.3 us (18%)
  between operations  13.5 us (14%)
  waiting for transfers between devices  13 us (14%)
  starting transfers between devices  6.92 us (7%)
  other arithmetic  4.6 us (5%)
  matrix products  2.08 us (2%)
    all_to_all x1, blocking collectives, local(): lax.all_to_all(outgoing, 'owner', split_axis=0, concat_axis=0, tiled=True)  32.9 us
    unnamed x7, local copies, waits for them, and re-layouts  6.68 us
    all_to_all x1, waiting for transfers between devices, local(): lax.all_to_all(outgoing_ranks, 'owner', split_axis=0, concat_axis=0, tile...  6.51 us
    all_to_all x1, waiting for transfers between devices, local(): lax.all_to_all(answers, 'owner', split_axis=0, concat_axis=0, tiled=True)  6.44 us
    gather x2, local copies, waits for them, and re-layouts, lookup_maxima(): return maxima[cluster_index, jnp.minimum(ranks, longest - 1)]  5.52 us
    all_to_all x1, starting transfers between devices, local(): lax.all_to_all(outgoing_ranks, 'owner', split_axis=0, concat_axis=0, tile...  3.59 us
    all_to_all x1, starting transfers between devices, local(): lax.all_to_all(answers, 'owner', split_axis=0, concat_axis=0, tiled=True)  3.33 us
    gather x1, local copies, waits for them, and re-layouts, local(): return returned.reshape(cluster_count * capacity)[slot_index]  2.51 us
  transfers between devices with their start and end apart: 3, of which 2 were waited for; matrix products, arithmetic and copies ran while one was open for 3% of the time, Pallas kernels for 0%

commit v1 on v0

--- a/solution.py
+++ b/solution.py
@@ -1,12 +1,221 @@
+import functools
+
 import jax
 import jax.numpy as jnp
 from jax import lax
+from jax.experimental import pallas as pl
+from jax.experimental.pallas import tpu as pltpu
 from jax.sharding import PartitionSpec as P
 
+MESH = pl.DeviceIdType.MESH
+EPSILON = 1e-06
+LANES = 128
+
+
+def flip(value, mask):
+    bit = 1
+    while bit <= mask:
+        if mask & bit:
+            value = value + bit * (1 - 2 * ((value // bit) % 2))
+        bit *= 2
+    return value
+
+
+def cluster_kernel(
+    count,
+    capacity,
+    emb_ref,
+    cluster_ref,
+    rank_ref,
+    out_ref,
+    send_rows,
+    rows,
+    send_ranks,
+    ranks,
+    send_best,
+    best,
+    row_send_sem,
+    row_recv_sem,
+    rank_send_sem,
+    rank_recv_sem,
+    best_send_sem,
+    best_recv_sem,
+):
+    row_count, width = emb_ref.shape
+    slots = count * capacity
+    per = LANES // capacity
+    owner = lax.axis_index("owner")
+    core = lax.axis_index("tile")
+    me = owner * 2 + core
+
+    def peer(k):
+        return {"owner": flip(owner, k // 2), "tile": flip(core, k % 2)}
+
+    barrier = pltpu.get_barrier_semaphore()
+    for k in range(1, count):
+        pl.semaphore_signal(barrier, inc=1, device_id=peer(k), device_id_type=MESH)
+
+    cluster = cluster_ref[...].reshape(1, row_count)
+    rank = rank_ref[...].reshape(1, row_count)
+    distance = cluster ^ me
+    member = distance == lax.broadcasted_iota(jnp.int32, (count, row_count), 0)
+    member_f = member.astype(jnp.float32)
+    member_b = member_f.astype(jnp.bfloat16)
+    before = (
+        lax.broadcasted_iota(jnp.int32, (row_count, row_count), 0)
+        < lax.broadcasted_iota(jnp.int32, (row_count, row_count), 1)
+    ).astype(jnp.float32).astype(jnp.bfloat16)
+    seen = jnp.dot(member_b, before, preferred_element_type=jnp.float32)
+    occurrence = jnp.sum(seen * member_f, axis=0, keepdims=True).astype(jnp.int32)
+    slot = distance * capacity + occurrence
+
+    lane_of = (slot % LANES) == lax.broadcasted_iota(jnp.int32, (LANES, row_count), 0)
+    lane_b = lane_of.astype(jnp.float32).astype(jnp.bfloat16)
+    high = (rank // 16 - slots // 16).astype(jnp.float32)
+    low = (rank % 16).astype(jnp.float32)
+    nt = (((1,), (1,)), ((), ()))
+    rank_high = lax.dot_general(
+        (member_f * high).astype(jnp.bfloat16), lane_b, nt, preferred_element_type=jnp.float32
+    )
+    rank_low = lax.dot_general(
+        (member_f * low).astype(jnp.bfloat16), lane_b, nt, preferred_element_type=jnp.float32
+    )
+    rank_rows = 16.0 * rank_high + rank_low
+    for k in range(count):
+        send_ranks[k] = rank_rows[k : k + 1, :]
+    ranks[0] = rank_rows[0:1, :]
+
+    values = emb_ref[...].astype(jnp.float32)
+    total = jnp.sum(values * values, axis=1, keepdims=True)
+    normed = (values * lax.rsqrt(total + EPSILON)).astype(jnp.bfloat16)
+
+    def place(first, size):
+        chosen = slot == first + lax.broadcasted_iota(jnp.int32, (size, row_count), 0)
+        chosen = chosen.astype(jnp.float32).astype(jnp.bfloat16)
+        return jnp.dot(chosen, normed, preferred_element_type=jnp.float32).astype(jnp.bfloat16)
+
+    def row_copy(k):
+        here = pl.ds(k * capacity, capacity)
+        return pltpu.make_async_remote_copy(
+            src_ref=send_rows.at[here],
+            dst_ref=rows.at[here],
+            send_sem=row_send_sem.at[k],
+            recv_sem=row_recv_sem.at[k],
+            device_id=peer(k),
+            device_id_type=MESH,
+        )
+
+    def rank_copy(k):
+        return pltpu.make_async_remote_copy(
+            src_ref=send_ranks.at[k],
+            dst_ref=ranks.at[k],
+            send_sem=rank_send_sem.at[k],
+            recv_sem=rank_recv_sem.at[k],
+            device_id=peer(k),
+            device_id_type=MESH,
+        )
+
+    def best_copy(k):
+        return pltpu.make_async_remote_copy(
+            src_ref=send_best.at[k // per],
+            dst_ref=best.at[k],
+            send_sem=best_send_sem.at[k],
+            recv_sem=best_recv_sem.at[k],
+            device_id=peer(k),
+            device_id_type=MESH,
+        )
+
+    half = slots // 2
+    send_rows[half:] = place(half, half)
+    pl.semaphore_wait(barrier, count - 1)
+    for k in range(count - 1, count // 2 - 1, -1):
+        row_copy(k).start()
+    for k in range(1, count):
+        rank_copy(k).start()
+    near = place(0, half)
+    send_rows[:half] = near
+    for k in range(count // 2 - 1, 0, -1):
+        row_copy(k).start()
+    rows[:capacity] = near[:capacity]
+
+    for k in range(1, count):
+        rank_copy(k).wait_recv()
+    blocks = slots // LANES
+    rank_lanes = jnp.concatenate(
+        [
+            sum(ranks[b * per + j] for j in range(per)) + float(slots)
+            for b in range(blocks)
+        ],
+        axis=0,
+    )
+    padded = jnp.concatenate([rank_lanes, jnp.zeros((LANES - blocks, LANES), jnp.float32)], axis=0)
+    turned = jnp.transpose(padded)
+
+    for k in range(1, count):
+        row_copy(k).wait_recv()
+    for q in range(blocks):
+        queries = rows[pl.ds(q * LANES, LANES)]
+        query_rank = rank_lanes[q : q + 1, :]
+        top = jnp.full((1, LANES), -1.0, jnp.float32)
+        scores = lax.dot_general(rows[...], queries, nt, preferred_element_type=jnp.float32)
+        for b in range(blocks):
+            part = scores[b * LANES : (b + 1) * LANES]
+            earlier = turned[:, b : b + 1] < query_rank
+            top = jnp.maximum(
+                top, jnp.max(jnp.where(earlier, part, -1.0), axis=0, keepdims=True)
+            )
+        send_best[q] = top
+        for k in range(q * per, (q + 1) * per):
+            if k:
+                best_copy(k).start()
+            else:
+                best[0] = top
+
+    for k in range(1, count):
+        best_copy(k).wait_recv()
+    answers = jnp.concatenate([best[k] for k in range(count)], axis=0)
+    spread = lax.dot_general(
+        jnp.transpose(answers),
+        member_f,
+        (((1,), (0,)), ((), ())),
+        precision=lax.Precision.HIGHEST,
+        preferred_element_type=jnp.float32,
+    )
+    picked = jnp.sum(jnp.where(lane_of, spread, 0.0), axis=0, keepdims=True)
+    out_ref[...] = picked.reshape(row_count)
+
+    for k in range(1, count):
+        row_copy(k).wait_send()
+        rank_copy(k).wait_send()
+        best_copy(k).wait_send()
+
+
+def fused(embeddings, cluster_of, rank_of, count):
+    row_count, width = embeddings.shape
+    capacity = 2 * row_count // count
+    slots = count * capacity
+    vmem = pl.BlockSpec(memory_space=pltpu.VMEM)
+    return pl.pallas_call(
+        functools.partial(cluster_kernel, count, capacity),
+        out_shape=jax.ShapeDtypeStruct((row_count,), jnp.float32),
+        in_specs=[vmem] * 3,
+        out_specs=vmem,
+        scratch_shapes=[
+            pltpu.VMEM((slots, width), jnp.bfloat16),
+            pltpu.VMEM((slots, width), jnp.bfloat16),
+            pltpu.VMEM((count, 1, LANES), jnp.float32),
+            pltpu.VMEM((count, 1, LANES), jnp.float32),
+            pltpu.VMEM((slots // LANES, 1, LANES), jnp.float32),
+            pltpu.VMEM((count, 1, LANES), jnp.float32),
+        ]
+        + [pltpu.SemaphoreType.DMA((count,))] * 6,
+        compiler_params=pltpu.CompilerParams(
+            collective_id=0, has_side_effects=True, vmem_limit_bytes=32 * 1024 * 1024
+        ),
+    )(embeddings, cluster_of, rank_of)
+
+
 CL_OWN = 2
-
-
-EPSILON = 1e-06
 
 
 def normalize_rows(embeddings):
@@ -45,7 +254,7 @@
     return jnp.stack(results)
 
 
-def local(embeddings, cluster_of, rank_of):
+def exchanged(embeddings, cluster_of, rank_of):
     row_count, feature_width = embeddings.shape
     owner_count = lax.axis_size("owner")
     core_count = lax.axis_size("tile")
@@ -96,6 +305,13 @@
     return returned.reshape(cluster_count * capacity)[slot_index]
 
 
+def local(embeddings, cluster_of, rank_of):
+    count = lax.axis_size("owner") * lax.axis_size("tile")
+    if (2 * embeddings.shape[0] // count) % 16 == 0:
+        return fused(embeddings, cluster_of, rank_of, count)
+    return exchanged(embeddings, cluster_of, rank_of)
+
+
 def solution(mesh):
     in_specs = (
         P(("groups", "owner", "tile"), None),

time: 94.3 us -> 42.6 us (0.45)
  Pallas kernels: 0 us -> 39.5 us
  blocking collectives: 36.5 us -> 0 us
  local copies, waits for them, and re-layouts: 17.3 us -> 2.96 us
  between operations: 13.5 us -> 0.01 us
  waiting for transfers between devices: 13 us -> 0 us
  starting transfers between devices: 6.92 us -> 0 us
  other arithmetic: 4.6 us -> 0 us
  matrix products: 2.08 us -> 0 us
    pallas_call x0 -> x1, Pallas kernels: none -> 39.5 us  [fused(): pl.pallas_call(functools.partial(cluster_kernel, count, capacity), out_sh...]
    all_to_all x1 -> x0, blocking collectives: 32.9 us -> none  [local(): lax.all_to_all(outgoing, 'owner', split_axis=0, concat_axis=0, tiled=True)]
    all_to_all x2 -> x0, waiting for transfers between devices: 12.9 us -> none  [the longest x1 6.51 us: local(): lax.all_to_all(outgoing_ranks, 'owner', split_axis=0, concat_axis=0, tile...]
    gather x3 -> x0, local copies, waits for them, and re-layouts: 8.03 us -> none  [the longest x2 5.52 us: lookup_maxima(): return maxima[cluster_index, jnp.minimum(ranks, longest - 1)]]
    all_to_all x2 -> x0, starting transfers between devices: 6.92 us -> none  [the longest x1 3.59 us: local(): lax.all_to_all(outgoing_ranks, 'owner', split_axis=0, concat_axis=0, tile...]
    unnamed x7, local copies, waits for them, and re-layouts: 6.68 us -> 2.96 us
    all_gather x2 -> x0, blocking collectives: 3.58 us -> none  [the longest x1 1.8 us: local(): lax.all_gather(arrived_ranks, 'tile', axis=0, tiled=True)]
    scatter x1 -> x0, other arithmetic: 2.47 us -> none  [local(): outgoing = jnp.zeros((cluster_count * capacity, feature_width), jnp.bfloa...]
  transfers between devices with their start and end apart: 3 -> 0, of which waited for: 2 -> 0; matrix products, arithmetic and copies ran while one was open for 3% -> 0% of each run, Pallas kernels for 0% -> 0%
where the time goes in v1:
time: 42.6 us; the launch traced here: 42.5 us
  Pallas kernels  39.5 us (93%)
  local copies, waits for them, and re-layouts  2.96 us (7%)
    pallas_call x1, Pallas kernels, fused(): pl.pallas_call(functools.partial(cluster_kernel, count, capacity), out_sh...  39.5 us
    unnamed x7, local copies, waits for them, and re-layouts  2.96 us

profile of v1, /device:TPU:0, one launch (start us, length us, event | category | flops | bytes accessed | tf_op | source)
XLA Modules:
  0.0 42.5 jit_solution(11231502593249359717)
XLA Ops:
  0.0 0.0 copy-start
  0.0 1.0 %copy-done = bf16[256,1024]{1,0:T(8,128)(2,1)S(1)} copy-done((bf16[256,1024]{1,0:T(8,128)(2,1)S(1)}, bf16[256,1024]{1,0:T(8,128)(2,1)}, u32[]{:S(2)}) %copy-start) | copy-done | bytes 524312
  1.0 0.0 copy-start.1
  1.0 0.7 %copy-done.1 = s32[256]{0:T(256)S(1)} copy-done((s32[256]{0:T(256)S(1)}, s32[256]{0:T(256)}, u32[]{:S(2)}) %copy-start.1) | copy-done | bytes 1048
  1.7 0.0 copy-start.2
  1.7 0.7 %copy-done.2 = s32[256]{0:T(256)S(1)} copy-done((s32[256]{0:T(256)S(1)}, s32[256]{0:T(256)}, u32[]{:S(2)}) %copy-start.2) | copy-done | bytes 1048
  2.4 39.5 %shard_map.37 = f32[256]{0:T(256)S(1)} custom-call(bf16[256,1024]{1,0:T(8,128)(2,1)S(1)} %copy-done, s32[256]{0:T(256)S(1)} %copy-done.1, s32[256]{0:T(256)S(1)} %copy-done.2), custom_call_target="tpu_custom_call" | custom-call | tf_op jit(solution)/shard_map/pallas_call | solution.py:198
  41.9 0.6 %copy.5 = f32[256]{0:T(256)} copy(f32[256]{0:T(256)S(1)} %shard_map.37) | data formatting | bytes 2048
Async XLA Ops:
  0.0 1.0 %copy-start = (bf16[256,1024]{1,0:T(8,128)(2,1)S(1)}, bf16[256,1024]{1,0:T(8,128)(2,1)}, u32[]{:S(2)}) copy-start(bf16[256,1024]{1,0:T(8,128)(2,1)} %emb_ref.1) | copy-start | bytes 1572868
  1.0 0.7 %copy-start.1 = (s32[256]{0:T(256)S(1)}, s32[256]{0:T(256)}, u32[]{:S(2)}) copy-start(s32[256]{0:T(256)} %cluster_ref.1) | copy-start | bytes 3076
  1.7 0.7 %copy-start.2 = (s32[256]{0:T(256)S(1)}, s32[256]{0:T(256)}, u32[]{:S(2)}) copy-start(s32[256]{0:T(256)} %rank_ref.1) | copy-start | bytes 3076

commit v2 on v1

--- a/solution.py
+++ b/solution.py
@@ -24,16 +24,21 @@
 def cluster_kernel(
     count,
     capacity,
+    emb_hbm,
+    cluster_hbm,
+    rank_hbm,
+    out_ref,
     emb_ref,
     cluster_ref,
     rank_ref,
-    out_ref,
     send_rows,
     rows,
+    normed,
     send_ranks,
     ranks,
     send_best,
     best,
+    load_sem,
     row_send_sem,
     row_recv_sem,
     rank_send_sem,
@@ -44,6 +49,7 @@
     row_count, width = emb_ref.shape
     slots = count * capacity
     per = LANES // capacity
+    blocks = slots // LANES
     owner = lax.axis_index("owner")
     core = lax.axis_index("tile")
     me = owner * 2 + core
@@ -51,48 +57,46 @@
     def peer(k):
         return {"owner": flip(owner, k // 2), "tile": flip(core, k % 2)}
 
+    loads = [
+        pltpu.make_async_copy(source, target, load_sem.at[i])
+        for i, (source, target) in enumerate(
+            [(cluster_hbm, cluster_ref), (rank_hbm, rank_ref), (emb_hbm, emb_ref)]
+        )
+    ]
+    for load in loads:
+        load.start()
     barrier = pltpu.get_barrier_semaphore()
-    for k in range(1, count):
+    for k in range(count - 1, 0, -1):
         pl.semaphore_signal(barrier, inc=1, device_id=peer(k), device_id_type=MESH)
 
+    loads[0].wait()
     cluster = cluster_ref[...].reshape(1, row_count)
-    rank = rank_ref[...].reshape(1, row_count)
     distance = cluster ^ me
     member = distance == lax.broadcasted_iota(jnp.int32, (count, row_count), 0)
     member_f = member.astype(jnp.float32)
     member_b = member_f.astype(jnp.bfloat16)
     before = (
-        lax.broadcasted_iota(jnp.int32, (row_count, row_count), 0)
-        < lax.broadcasted_iota(jnp.int32, (row_count, row_count), 1)
-    ).astype(jnp.float32).astype(jnp.bfloat16)
+        (
+            lax.broadcasted_iota(jnp.int32, (row_count, row_count), 0)
+            < lax.broadcasted_iota(jnp.int32, (row_count, row_count), 1)
+        )
+        .astype(jnp.float32)
+        .astype(jnp.bfloat16)
+    )
     seen = jnp.dot(member_b, before, preferred_element_type=jnp.float32)
     occurrence = jnp.sum(seen * member_f, axis=0, keepdims=True).astype(jnp.int32)
     slot = distance * capacity + occurrence
-
-    lane_of = (slot % LANES) == lax.broadcasted_iota(jnp.int32, (LANES, row_count), 0)
-    lane_b = lane_of.astype(jnp.float32).astype(jnp.bfloat16)
-    high = (rank // 16 - slots // 16).astype(jnp.float32)
-    low = (rank % 16).astype(jnp.float32)
     nt = (((1,), (1,)), ((), ()))
-    rank_high = lax.dot_general(
-        (member_f * high).astype(jnp.bfloat16), lane_b, nt, preferred_element_type=jnp.float32
-    )
-    rank_low = lax.dot_general(
-        (member_f * low).astype(jnp.bfloat16), lane_b, nt, preferred_element_type=jnp.float32
-    )
-    rank_rows = 16.0 * rank_high + rank_low
-    for k in range(count):
-        send_ranks[k] = rank_rows[k : k + 1, :]
-    ranks[0] = rank_rows[0:1, :]
-
-    values = emb_ref[...].astype(jnp.float32)
-    total = jnp.sum(values * values, axis=1, keepdims=True)
-    normed = (values * lax.rsqrt(total + EPSILON)).astype(jnp.bfloat16)
-
-    def place(first, size):
-        chosen = slot == first + lax.broadcasted_iota(jnp.int32, (size, row_count), 0)
+
+    def block_rows(b, n=1):
+        return pl.ds(b * LANES, n * LANES)
+
+    def place(b, n=1):
+        size = n * LANES
+        chosen = slot == b * LANES + lax.broadcasted_iota(jnp.int32, (size, row_count), 0)
         chosen = chosen.astype(jnp.float32).astype(jnp.bfloat16)
-        return jnp.dot(chosen, normed, preferred_element_type=jnp.float32).astype(jnp.bfloat16)
+        placed = jnp.dot(chosen, emb_ref[...], preferred_element_type=jnp.float32)
+        send_rows[block_rows(b, n)] = placed.astype(jnp.bfloat16)
 
     def row_copy(k):
         here = pl.ds(k * capacity, capacity)
@@ -125,52 +129,103 @@
             device_id_type=MESH,
         )
 
-    half = slots // 2
-    send_rows[half:] = place(half, half)
+    def start_rows(b):
+        for k in range((b + 1) * per - 1, b * per - 1, -1):
+            if k:
+                row_copy(k).start()
+
+    loads[2].wait()
+    place(blocks - 1)
     pl.semaphore_wait(barrier, count - 1)
-    for k in range(count - 1, count // 2 - 1, -1):
-        row_copy(k).start()
-    for k in range(1, count):
+    start_rows(blocks - 1)
+    place(blocks - 2)
+    start_rows(blocks - 2)
+
+    loads[1].wait()
+    rank = rank_ref[...].reshape(1, row_count)
+    lane_of = (slot % LANES) == lax.broadcasted_iota(jnp.int32, (LANES, row_count), 0)
+    lane_b = lane_of.astype(jnp.float32).astype(jnp.bfloat16)
+    high = (rank // 16 - slots // 16).astype(jnp.float32)
+    low = (rank % 16).astype(jnp.float32)
+    rank_high = lax.dot_general(
+        (member_f * high).astype(jnp.bfloat16), lane_b, nt, preferred_element_type=jnp.float32
+    )
+    rank_low = lax.dot_general(
+        (member_f * low).astype(jnp.bfloat16), lane_b, nt, preferred_element_type=jnp.float32
+    )
+    rank_rows = 16.0 * rank_high + rank_low
+    for k in range(count):
+        send_ranks[k] = rank_rows[k : k + 1, :]
+    for k in range(count - 1, 0, -1):
         rank_copy(k).start()
-    near = place(0, half)
-    send_rows[:half] = near
-    for k in range(count // 2 - 1, 0, -1):
-        row_copy(k).start()
-    rows[:capacity] = near[:capacity]
+    ranks[0] = rank_rows[0:1, :]
+
+    place(0, blocks - 2)
+    for b in range(blocks - 3, -1, -1):
+        start_rows(b)
+    rows[:capacity] = send_rows[:capacity]
+
+    def arrive(b, n=1):
+        for k in range((b + n) * per - 1, b * per - 1, -1):
+            if k:
+                row_copy(k).wait_recv()
+        values = rows[block_rows(b, n)].astype(jnp.float32)
+        total = jnp.sum(values * values, axis=1, keepdims=True)
+        normed[block_rows(b, n)] = (values * lax.rsqrt(total + EPSILON)).astype(jnp.bfloat16)
 
     for k in range(1, count):
         rank_copy(k).wait_recv()
-    blocks = slots // LANES
-    rank_lanes = jnp.concatenate(
-        [
-            sum(ranks[b * per + j] for j in range(per)) + float(slots)
-            for b in range(blocks)
-        ],
-        axis=0,
-    )
-    padded = jnp.concatenate([rank_lanes, jnp.zeros((LANES - blocks, LANES), jnp.float32)], axis=0)
-    turned = jnp.transpose(padded)
-
-    for k in range(1, count):
-        row_copy(k).wait_recv()
-    for q in range(blocks):
-        queries = rows[pl.ds(q * LANES, LANES)]
-        query_rank = rank_lanes[q : q + 1, :]
-        top = jnp.full((1, LANES), -1.0, jnp.float32)
-        scores = lax.dot_general(rows[...], queries, nt, preferred_element_type=jnp.float32)
-        for b in range(blocks):
-            part = scores[b * LANES : (b + 1) * LANES]
-            earlier = turned[:, b : b + 1] < query_rank
-            top = jnp.maximum(
-                top, jnp.max(jnp.where(earlier, part, -1.0), axis=0, keepdims=True)
-            )
-        send_best[q] = top
-        for k in range(q * per, (q + 1) * per):
+    rank_lanes = [
+        sum(ranks[b * per + j] for j in range(per)) + float(slots) for b in range(blocks)
+    ]
+    turned = jnp.transpose(
+        jnp.concatenate(rank_lanes + [jnp.zeros((LANES - blocks, LANES), jnp.float32)], axis=0)
+    )
+    tops = [jnp.full((1, LANES), -1.0, jnp.float32) for _ in range(blocks)]
+
+    def score(first_key, keys, first_query, queries):
+        scores = lax.dot_general(
+            normed[block_rows(first_key, keys)],
+            normed[block_rows(first_query, queries)],
+            nt,
+            preferred_element_type=jnp.float32,
+        )
+        for q in range(queries):
+            for b in range(keys):
+                part = scores[b * LANES : (b + 1) * LANES, q * LANES : (q + 1) * LANES]
+                key = first_key + b
+                query = first_query + q
+                earlier = turned[:, key : key + 1] < rank_lanes[query]
+                found = jnp.max(jnp.where(earlier, part, -1.0), axis=0, keepdims=True)
+                tops[query] = jnp.maximum(tops[query], found)
+
+    def answer(b):
+        send_best[b] = tops[b]
+        for k in range((b + 1) * per - 1, b * per - 1, -1):
             if k:
                 best_copy(k).start()
             else:
-                best[0] = top
-
+                best[0] = tops[b]
+
+    near = blocks - 2
+    arrive(0, near)
+    score(0, near, 0, near)
+    arrive(near + 1)
+    score(0, near, near + 1, 1)
+    score(near + 1, 1, near + 1, 1)
+    score(near + 1, 1, 0, near)
+    arrive(near)
+    score(near, 1, near + 1, 1)
+    answer(near + 1)
+    score(0, blocks, near, 1)
+    answer(near)
+    score(near, 1, 0, near)
+    for b in range(near - 1, -1, -1):
+        answer(b)
+
+    for k in range(1, count):
+        row_copy(k).wait_send()
+        rank_copy(k).wait_send()
     for k in range(1, count):
         best_copy(k).wait_recv()
     answers = jnp.concatenate([best[k] for k in range(count)], axis=0)
@@ -183,10 +238,7 @@
     )
     picked = jnp.sum(jnp.where(lane_of, spread, 0.0), axis=0, keepdims=True)
     out_ref[...] = picked.reshape(row_count)
-
     for k in range(1, count):
-        row_copy(k).wait_send()
-        rank_copy(k).wait_send()
         best_copy(k).wait_send()
 
 
@@ -194,23 +246,27 @@
     row_count, width = embeddings.shape
     capacity = 2 * row_count // count
     slots = count * capacity
-    vmem = pl.BlockSpec(memory_space=pltpu.VMEM)
     return pl.pallas_call(
         functools.partial(cluster_kernel, count, capacity),
         out_shape=jax.ShapeDtypeStruct((row_count,), jnp.float32),
-        in_specs=[vmem] * 3,
-        out_specs=vmem,
+        in_specs=[pl.BlockSpec(memory_space=pl.ANY)] * 3,
+        out_specs=pl.BlockSpec(memory_space=pltpu.VMEM),
         scratch_shapes=[
+            pltpu.VMEM((row_count, width), jnp.bfloat16),
+            pltpu.VMEM((row_count,), jnp.int32),
+            pltpu.VMEM((row_count,), jnp.int32),
+            pltpu.VMEM((slots, width), jnp.bfloat16),
             pltpu.VMEM((slots, width), jnp.bfloat16),
             pltpu.VMEM((slots, width), jnp.bfloat16),
             pltpu.VMEM((count, 1, LANES), jnp.float32),
             pltpu.VMEM((count, 1, LANES), jnp.float32),
             pltpu.VMEM((slots // LANES, 1, LANES), jnp.float32),
             pltpu.VMEM((count, 1, LANES), jnp.float32),
+            pltpu.SemaphoreType.DMA((3,)),
         ]
         + [pltpu.SemaphoreType.DMA((count,))] * 6,
         compiler_params=pltpu.CompilerParams(
-            collective_id=0, has_side_effects=True, vmem_limit_bytes=32 * 1024 * 1024
+            collective_id=0, has_side_effects=True, vmem_limit_bytes=48 * 1024 * 1024
         ),
     )(embeddings, cluster_of, rank_of)
 

time: 42.6 us -> 42.1 us (0.988)
  Pallas kernels: 39.5 us -> 38.9 us
    pallas_call x1, Pallas kernels: 39.5 us -> 38.9 us  [fused(): pl.pallas_call(functools.partial(cluster_kernel, count, capacity), out_sh...]
where the time goes in v2:
time: 42.1 us; the launch traced here: 41.9 us
  Pallas kernels  38.9 us (92%)
  local copies, waits for them, and re-layouts  2.96 us (7%)
    pallas_call x1, Pallas kernels, fused(): pl.pallas_call(functools.partial(cluster_kernel, count, capacity), out_sh...  38.9 us
    unnamed x7, local copies, waits for them, and re-layouts  2.96 us

profile of v2, /device:TPU:0, one launch (start us, length us, event | category | flops | bytes accessed | tf_op | source)
XLA Modules:
  0.0 41.9 jit_solution(3268316218213915720)
XLA Ops:
  0.0 0.0 copy-start
  0.0 1.0 %copy-done = bf16[256,1024]{1,0:T(8,128)(2,1)S(1)} copy-done((bf16[256,1024]{1,0:T(8,128)(2,1)S(1)}, bf16[256,1024]{1,0:T(8,128)(2,1)}, u32[]{:S(2)}) %copy-start) | copy-done | bytes 524312
  1.0 0.0 copy-start.1
  1.0 0.7 %copy-done.1 = s32[256]{0:T(256)S(1)} copy-done((s32[256]{0:T(256)S(1)}, s32[256]{0:T(256)}, u32[]{:S(2)}) %copy-start.1) | copy-done | bytes 1048
  1.7 0.0 copy-start.2
  1.7 0.7 %copy-done.2 = s32[256]{0:T(256)S(1)} copy-done((s32[256]{0:T(256)S(1)}, s32[256]{0:T(256)}, u32[]{:S(2)}) %copy-start.2) | copy-done | bytes 1048
  2.4 38.9 %shard_map.37 = f32[256]{0:T(256)S(1)} custom-call(bf16[256,1024]{1,0:T(8,128)(2,1)S(1)} %copy-done, s32[256]{0:T(256)S(1)} %copy-done.1, s32[256]{0:T(256)S(1)} %copy-done.2), custom_call_target="tpu_custom_call" | custom-call | tf_op jit(solution)/shard_map/pallas_call | solution.py:249
  41.3 0.6 %copy.5 = f32[256]{0:T(256)} copy(f32[256]{0:T(256)S(1)} %shard_map.37) | data formatting | bytes 2048
Async XLA Ops:
  0.0 1.0 %copy-start = (bf16[256,1024]{1,0:T(8,128)(2,1)S(1)}, bf16[256,1024]{1,0:T(8,128)(2,1)}, u32[]{:S(2)}) copy-start(bf16[256,1024]{1,0:T(8,128)(2,1)} %emb_hbm.1) | copy-start | bytes 1572868
  1.0 0.7 %copy-start.1 = (s32[256]{0:T(256)S(1)}, s32[256]{0:T(256)}, u32[]{:S(2)}) copy-start(s32[256]{0:T(256)} %cluster_hbm.1) | copy-start | bytes 3076
  1.7 0.7 %copy-start.2 = (s32[256]{0:T(256)S(1)}, s32[256]{0:T(256)}, u32[]{:S(2)}) copy-start(s32[256]{0:T(256)} %rank_hbm.1) | copy-start | bytes 3076

commit v3 on v2

--- a/solution.py
+++ b/solution.py
@@ -134,13 +134,6 @@
             if k:
                 row_copy(k).start()
 
-    loads[2].wait()
-    place(blocks - 1)
-    pl.semaphore_wait(barrier, count - 1)
-    start_rows(blocks - 1)
-    place(blocks - 2)
-    start_rows(blocks - 2)
-
     loads[1].wait()
     rank = rank_ref[...].reshape(1, row_count)
     lane_of = (slot % LANES) == lax.broadcasted_iota(jnp.int32, (LANES, row_count), 0)
@@ -156,9 +149,16 @@
     rank_rows = 16.0 * rank_high + rank_low
     for k in range(count):
         send_ranks[k] = rank_rows[k : k + 1, :]
+    ranks[0] = rank_rows[0:1, :]
+
+    loads[2].wait()
+    place(blocks - 1)
+    pl.semaphore_wait(barrier, count - 1)
     for k in range(count - 1, 0, -1):
         rank_copy(k).start()
-    ranks[0] = rank_rows[0:1, :]
+    start_rows(blocks - 1)
+    place(blocks - 2)
+    start_rows(blocks - 2)
 
     place(0, blocks - 2)
     for b in range(blocks - 3, -1, -1):
@@ -265,9 +265,7 @@
             pltpu.SemaphoreType.DMA((3,)),
         ]
         + [pltpu.SemaphoreType.DMA((count,))] * 6,
-        compiler_params=pltpu.CompilerParams(
-            collective_id=0, has_side_effects=True, vmem_limit_bytes=48 * 1024 * 1024
-        ),
+        compiler_params=pltpu.CompilerParams(collective_id=0, has_side_effects=True),
     )(embeddings, cluster_of, rank_of)
 
 

time: 42.1 us -> 38.5 us (0.914)
  Pallas kernels: 38.9 us -> 37.1 us
  local copies, waits for them, and re-layouts: 2.96 us -> 1.24 us
    pallas_call x1, Pallas kernels: 38.9 us -> 37.1 us  [fused(): pl.pallas_call(functools.partial(cluster_kernel, count, capacity), out_sh...]
    unnamed x7 -> x1, local copies, waits for them, and re-layouts: 2.96 us -> 1.24 us
where the time goes in v3:
time: 38.5 us; the launch traced here: 38.3 us
  Pallas kernels  37.1 us (96%)
  local copies, waits for them, and re-layouts  1.24 us (3%)
    pallas_call x1, Pallas kernels, fused(): pl.pallas_call(functools.partial(cluster_kernel, count, capacity), out_sh...  37.1 us
    unnamed x1, local copies, waits for them, and re-layouts  1.24 us

profile of v3, /device:TPU:0, one launch (start us, length us, event | category | flops | bytes accessed | tf_op | source)
XLA Modules:
  0.0 38.3 jit_solution(7728288826486186838)
XLA Ops:
  0.0 37.1 %shard_map.37 = f32[256]{0:T(256)} custom-call(bf16[256,1024]{1,0:T(8,128)(2,1)} %emb_hbm.1, s32[256]{0:T(256)} %cluster_hbm.1, s32[256]{0:T(256)} %rank_hbm.1), custom_call_target="tpu_custom_call" | custom-call | tf_op jit(solution)/shard_map/pallas_call | solution.py:249
  37.1 1.2 %copy.5 = f32[256]{0:T(256)} copy(f32[256]{0:T(256)} %shard_map.37) | data formatting | bytes 2048

commit v4 on v3

--- a/solution.py
+++ b/solution.py
@@ -95,7 +95,7 @@
         size = n * LANES
         chosen = slot == b * LANES + lax.broadcasted_iota(jnp.int32, (size, row_count), 0)
         chosen = chosen.astype(jnp.float32).astype(jnp.bfloat16)
-        placed = jnp.dot(chosen, emb_ref[...], preferred_element_type=jnp.float32)
+        placed = jnp.dot(chosen, normed[...], preferred_element_type=jnp.float32)
         send_rows[block_rows(b, n)] = placed.astype(jnp.bfloat16)
 
     def row_copy(k):
@@ -152,13 +152,17 @@
     ranks[0] = rank_rows[0:1, :]
 
     loads[2].wait()
+    values = emb_ref[...].astype(jnp.float32)
+    total = jnp.sum(values * values, axis=1, keepdims=True)
+    normed[...] = (values * lax.rsqrt(total + EPSILON)).astype(jnp.bfloat16)
     place(blocks - 1)
     pl.semaphore_wait(barrier, count - 1)
     for k in range(count - 1, 0, -1):
         rank_copy(k).start()
-    start_rows(blocks - 1)
     place(blocks - 2)
-    start_rows(blocks - 2)
+    for j in range(per - 1, -1, -1):
+        row_copy((blocks - 1) * per + j).start()
+        row_copy((blocks - 2) * per + j).start()
 
     place(0, blocks - 2)
     for b in range(blocks - 3, -1, -1):
@@ -169,9 +173,6 @@
         for k in range((b + n) * per - 1, b * per - 1, -1):
             if k:
                 row_copy(k).wait_recv()
-        values = rows[block_rows(b, n)].astype(jnp.float32)
-        total = jnp.sum(values * values, axis=1, keepdims=True)
-        normed[block_rows(b, n)] = (values * lax.rsqrt(total + EPSILON)).astype(jnp.bfloat16)
 
     for k in range(1, count):
         rank_copy(k).wait_recv()
@@ -185,8 +186,8 @@
 
     def score(first_key, keys, first_query, queries):
         scores = lax.dot_general(
-            normed[block_rows(first_key, keys)],
-            normed[block_rows(first_query, queries)],
+            rows[block_rows(first_key, keys)],
+            rows[block_rows(first_query, queries)],
             nt,
             preferred_element_type=jnp.float32,
         )
@@ -257,7 +258,7 @@
             pltpu.VMEM((row_count,), jnp.int32),
             pltpu.VMEM((slots, width), jnp.bfloat16),
             pltpu.VMEM((slots, width), jnp.bfloat16),
-            pltpu.VMEM((slots, width), jnp.bfloat16),
+            pltpu.VMEM((row_count, width), jnp.bfloat16),
             pltpu.VMEM((count, 1, LANES), jnp.float32),
             pltpu.VMEM((count, 1, LANES), jnp.float32),
             pltpu.VMEM((slots // LANES, 1, LANES), jnp.float32),

time: 38.5 us -> 37.8 us (0.982)
  Pallas kernels: 37.1 us -> 36.4 us
    pallas_call x1, Pallas kernels: 37.1 us -> 36.4 us  [fused(): pl.pallas_call(functools.partial(cluster_kernel, count, capacity), out_sh...]
where the time goes in v4:
time: 37.8 us; the launch traced here: 37.7 us
  Pallas kernels  36.4 us (96%)
  local copies, waits for them, and re-layouts  1.24 us (3%)
    pallas_call x1, Pallas kernels, fused(): pl.pallas_call(functools.partial(cluster_kernel, count, capacity), out_sh...  36.4 us
    unnamed x1, local copies, waits for them, and re-layouts  1.24 us

profile of v4, /device:TPU:0, one launch (start us, length us, event | category | flops | bytes accessed | tf_op | source)
XLA Modules:
  0.0 37.7 jit_solution(14435750370686068337)
XLA Ops:
  0.0 36.4 %shard_map.37 = f32[256]{0:T(256)} custom-call(bf16[256,1024]{1,0:T(8,128)(2,1)} %emb_hbm.1, s32[256]{0:T(256)} %cluster_hbm.1, s32[256]{0:T(256)} %rank_hbm.1), custom_call_target="tpu_custom_call" | custom-call | tf_op jit(solution)/shard_map/pallas_call | solution.py:250
  36.4 1.2 %copy.5 = f32[256]{0:T(256)} copy(f32[256]{0:T(256)} %shard_map.37) | data formatting | bytes 2048

commit v5 on v4

--- a/solution.py
+++ b/solution.py
@@ -63,11 +63,11 @@
             [(cluster_hbm, cluster_ref), (rank_hbm, rank_ref), (emb_hbm, emb_ref)]
         )
     ]
-    for load in loads:
-        load.start()
     barrier = pltpu.get_barrier_semaphore()
     for k in range(count - 1, 0, -1):
         pl.semaphore_signal(barrier, inc=1, device_id=peer(k), device_id_type=MESH)
+    for load in loads:
+        load.start()
 
     loads[0].wait()
     cluster = cluster_ref[...].reshape(1, row_count)
@@ -228,19 +228,19 @@
         row_copy(k).wait_send()
         rank_copy(k).wait_send()
     for k in range(1, count):
+        best_copy(k).wait_send()
+    for k in range(1, count):
         best_copy(k).wait_recv()
     answers = jnp.concatenate([best[k] for k in range(count)], axis=0)
-    spread = lax.dot_general(
-        jnp.transpose(answers),
-        member_f,
-        (((1,), (0,)), ((), ())),
-        precision=lax.Precision.HIGHEST,
-        preferred_element_type=jnp.float32,
-    )
+    turned_answers = jnp.transpose(answers)
+    parts = []
+    for _ in range(3):
+        part = turned_answers.astype(jnp.bfloat16)
+        turned_answers = turned_answers - part.astype(jnp.float32)
+        parts.append(jnp.dot(part, member_b, preferred_element_type=jnp.float32))
+    spread = (parts[2] + parts[1]) + parts[0]
     picked = jnp.sum(jnp.where(lane_of, spread, 0.0), axis=0, keepdims=True)
     out_ref[...] = picked.reshape(row_count)
-    for k in range(1, count):
-        best_copy(k).wait_send()
 
 
 def fused(embeddings, cluster_of, rank_of, count):

time: 37.8 us -> 37.7 us (level)
  no operation moved by 1% of the time
where the time goes in v5:
time: 37.7 us; the launch traced here: 37.6 us
  Pallas kernels  36.3 us (96%)
  local copies, waits for them, and re-layouts  1.24 us (3%)
    pallas_call x1, Pallas kernels, fused(): pl.pallas_call(functools.partial(cluster_kernel, count, capacity), out_sh...  36.3 us
    unnamed x1, local copies, waits for them, and re-layouts  1.24 us

profile of v5, /device:TPU:0, one launch (start us, length us, event | category | flops | bytes accessed | tf_op | source)
XLA Modules:
  0.0 37.6 jit_solution(11809279678290632179)
XLA Ops:
  0.0 36.3 %shard_map.37 = f32[256]{0:T(256)} custom-call(bf16[256,1024]{1,0:T(8,128)(2,1)} %emb_hbm.1, s32[256]{0:T(256)} %cluster_hbm.1, s32[256]{0:T(256)} %rank_hbm.1), custom_call_target="tpu_custom_call" | custom-call | tf_op jit(solution)/shard_map/pallas_call | solution.py:250
  36.3 1.2 %copy.5 = f32[256]{0:T(256)} copy(f32[256]{0:T(256)} %shard_map.37) | data formatting | bytes 2048

commit v6 on v5

--- a/solution.py
+++ b/solution.py
@@ -155,11 +155,10 @@
     values = emb_ref[...].astype(jnp.float32)
     total = jnp.sum(values * values, axis=1, keepdims=True)
     normed[...] = (values * lax.rsqrt(total + EPSILON)).astype(jnp.bfloat16)
-    place(blocks - 1)
+    place(blocks - 2, 2)
     pl.semaphore_wait(barrier, count - 1)
     for k in range(count - 1, 0, -1):
         rank_copy(k).start()
-    place(blocks - 2)
     for j in range(per - 1, -1, -1):
         row_copy((blocks - 1) * per + j).start()
         row_copy((blocks - 2) * per + j).start()

time: 37.7 us -> 37.6 us (level)
  no operation moved by 1% of the time
where the time goes in v6:
time: 37.6 us; the launch traced here: 37.5 us
  Pallas kernels  36.2 us (96%)
  local copies, waits for them, and re-layouts  1.24 us (3%)
    pallas_call x1, Pallas kernels, fused(): pl.pallas_call(functools.partial(cluster_kernel, count, capacity), out_sh...  36.2 us
    unnamed x1, local copies, waits for them, and re-layouts  1.24 us

profile of v6, /device:TPU:0, one launch (start us, length us, event | category | flops | bytes accessed | tf_op | source)
XLA Modules:
  0.0 37.5 jit_solution(5641181757164396349)
XLA Ops:
  0.0 36.2 %shard_map.37 = f32[256]{0:T(256)} custom-call(bf16[256,1024]{1,0:T(8,128)(2,1)} %emb_hbm.1, s32[256]{0:T(256)} %cluster_hbm.1, s32[256]{0:T(256)} %rank_hbm.1), custom_call_target="tpu_custom_call" | custom-call | tf_op jit(solution)/shard_map/pallas_call | solution.py:249
  36.2 1.2 %copy.5 = f32[256]{0:T(256)} copy(f32[256]{0:T(256)} %shard_map.37) | data formatting | bytes 2048
